TPU v7x, 128 devices: a whole 4x4x4 slice. The times are simulated.
128 devices in a mesh: dp: 16 (over y_lo, x, core), tensor: 8 (over y_hi, z).
Axes of the slice: x: 4, y: 4 (y_hi: 2, y_lo: 2; y = y_hi * 2 + y_lo), z: 4, core: 2. Of those that a mesh axis runs over, the one named last changes fastest.
Arguments:
- picture_encoder_result: bfloat16 [5632, 1024], P('dp'), may hold values from -0.59765625 to 0.59765625
- sentence_encoder_result: bfloat16 [22528, 1024], P(('dp', 'tensor')), may hold values from -0.59765625 to 0.59765625
- picture_projector_matrix: bfloat16 [1024, 1024], P(None, 'tensor'), may hold values from -0.1875 to 0.1875
- sentence_projector_matrix: bfloat16 [1024, 1024], P(None, 'tensor'), may hold values from -0.1875 to 0.1875
- sentences_for_picture: int32 [5632], replicated, may hold values from 1 to 8, 22528 in all
- sharpness_factor: float32 [1], replicated, may hold values from 30 to 60
- score_offset_term: float32 [1], replicated, may hold values from -8 to -4
Outputs:
- grad_img: bfloat16 [5632, 1024], P('dp', 'tensor')
- grad_cap: bfloat16 [22528, 1024], P(('dp', 'tensor'))
Inputs may be any that keep to these rules, and one draw needn't show every extreme that they name: The counts sum to 22528; the captions of image m are the consecutive rows start[m] to start[m] + sentences_for_picture[m] - 1 of sentence_encoder_result, where start[m] is the sum of the counts of images before m; some image has 8.
All inputs are finite; a program needn't handle non-finite values.
Results may differ from a plain program's by a relative error of at most 0.014.
Values may be sent and summed in bfloat16 or wider, within the bound.
A program may use at most 64 MiB of HBM per device.

v0:
```python
import jax
import jax.numpy as jnp
from jax import lax
from jax.sharding import PartitionSpec as P

epsilon = 1e-06


def passed_along(value, axis, steps):
    count = lax.axis_size(axis)
    pairs = [(source, (source + steps) % count) for source in range(count)]
    return lax.ppermute(value, axis, pairs)


def embed(features, loss_multiplier):
    raw = jnp.dot(features, loss_multiplier, preferred_element_type=jnp.float32)
    scale = lax.rsqrt(jnp.sum(raw * raw, axis=1, keepdims=True) + epsilon)
    return (raw * scale, scale)


def scaling_factor(
    similarity_matrix,
    other_begin_list,
    sentence_tally_later,
    other_position,
    scaled_sharpness,
    displacement,
):
    raw_similarity = scaled_sharpness * similarity_matrix + displacement
    inside = (other_position >= other_begin_list) & (
        other_position < other_begin_list + sentence_tally_later
    )
    match_polarity = jnp.where(inside, 1.0, -1.0)
    loss_multiplier = jnp.where(inside, 1.0 / sentence_tally_later.astype(jnp.float32), 1.0)
    return (
        scaled_sharpness
        * (-match_polarity * loss_multiplier * jax.nn.sigmoid(-match_polarity * raw_similarity))
    ).astype(jnp.bfloat16)


def unit_back(grad, unit, scale):
    return scale * (grad - unit * jnp.sum(unit * grad, axis=1, keepdims=True))


def divided_product(values, loss_multiplier):
    upper = lax.optimization_barrier(values.astype(jnp.bfloat16))
    lower = (values - upper.astype(jnp.float32)).astype(jnp.bfloat16)
    first = jnp.einsum("me,de->md", upper, loss_multiplier, preferred_element_type=jnp.float32)
    return first + jnp.einsum(
        "me,de->md", lower, loss_multiplier, preferred_element_type=jnp.float32
    )


def body(
    picture_encoder_result,
    sentence_encoder_result,
    picture_projector_matrix,
    sentence_projector_matrix,
    sentences_for_picture,
    sharpness_factor,
    score_offset_term,
):
    full_img, full_cap = (
        lax.all_gather(picture_projector_matrix, "tensor", axis=1, tiled=True),
        lax.all_gather(sentence_projector_matrix, "tensor", axis=1, tiled=True),
    )
    img_unit, img_scale = embed(picture_encoder_result, full_img)
    cap_unit, cap_scale = embed(sentence_encoder_result, full_cap)
    img_z = img_unit.astype(jnp.bfloat16)
    cap_z = cap_unit.astype(jnp.bfloat16)
    scaled_sharpness = sharpness_factor[0]
    displacement = score_offset_term[0]
    ends = jnp.cumsum(sentences_for_picture)
    starts = ends - sentences_for_picture
    cycle_count = lax.axis_size("dp")
    tensor_count = lax.axis_size("tensor")
    cycle_pos = lax.axis_index("dp")
    tensor_pos = lax.axis_index("tensor")
    img_rows = picture_encoder_result.shape[0]
    cap_rows = sentence_encoder_result.shape[0]
    width = img_z.shape[1]
    row_iota = jnp.arange(cap_rows, dtype=jnp.int32)
    sentence_number = (cycle_pos * tensor_count + tensor_pos) * cap_rows + row_iota

    def block_of(anchor):
        first = anchor * img_rows
        group_begin_list = lax.dynamic_slice_in_dim(starts, first, img_rows)
        group_sizes_list = lax.dynamic_slice_in_dim(sentences_for_picture, first, img_rows)
        return (group_begin_list, group_sizes_list)

    def image_tile(block_z, anchor):
        group_begin_list, group_sizes_list = block_of(anchor)
        similarity_matrix = jnp.einsum(
            "me,ce->mc", block_z, cap_z, preferred_element_type=jnp.float32
        )
        return scaling_factor(
            similarity_matrix,
            group_begin_list[:, None],
            group_sizes_list[:, None],
            sentence_number[None, :],
            scaled_sharpness,
            displacement,
        )

    def step(turn, state):
        block_z, carried, cap_grad = state
        anchor = (cycle_pos - turn) % cycle_count
        pair_factor = image_tile(block_z, anchor)
        cap_grad = cap_grad + jnp.einsum(
            "mc,me->ce", pair_factor, block_z, preferred_element_type=jnp.float32
        )
        carried = carried + jnp.dot(pair_factor, cap_z, preferred_element_type=jnp.float32)
        carried = passed_along(carried.astype(jnp.bfloat16), "dp", 1).astype(carried.dtype)
        block_z = passed_along(block_z, "dp", 1)
        return (block_z, carried, cap_grad)

    start_state = (
        img_z,
        jnp.zeros((img_rows, width), jnp.float32),
        jnp.zeros((cap_rows, width), jnp.float32),
    )
    unused, img_grad, cap_grad = lax.fori_loop(0, cycle_count, step, start_state)
    img_back = unit_back(img_grad, img_unit, img_scale)
    img_part = divided_product(img_back, full_img)
    grad_img = lax.psum_scatter(
        img_part.astype(jnp.bfloat16), "tensor", scatter_dimension=1, tiled=True
    )
    cap_back = unit_back(cap_grad, cap_unit, cap_scale)
    grad_cap = divided_product(cap_back, full_cap)
    return (grad_img, grad_cap.astype(jnp.bfloat16))


def solution(mesh):
    in_specs = (
        P("dp", None),
        P(("dp", "tensor"), None),
        P(None, "tensor"),
        P(None, "tensor"),
        P(),
        P(),
        P(),
    )
    out_specs = (P("dp", "tensor"), P(("dp", "tensor"), None))
    return jax.shard_map(body, mesh=mesh, in_specs=in_specs, out_specs=out_specs, check_vma=False)
```

profile of v0, /device:TPU:0, one launch (start us, length us, event | category | flops | bytes accessed | tf_op | source)
XLA Modules:
  0.0 632.3 jit_solution(152464883537165580)
XLA Ops:
  10.8 56.4 %all-gather.5.cloned.1.call-done = bf16[1024,1024]{1,0:T(8,128)(2,1)} async-done(((bf16[1024,128]{1,0:T(8,128)(2,1)}), bf16[1024,1024]{1,0:T(8,128)(2,1)}) %all-gather.5.cloned.1.call-update) | async-done | bytes 2097168 | tf_op jit(solution)/shard_map/all_gather | solution.py:65
  69.7 52.2 %all-gather.3.cloned.1.call-done = bf16[1024,1024]{1,0:T(8,128)(2,1)} async-done(((bf16[1024,128]{1,0:T(8,128)(2,1)}), bf16[1024,1024]{1,0:T(8,128)(2,1)}) %all-gather.3.cloned.1.call-update) | async-done | bytes 2097168 | tf_op jit(solution)/shard_map/all_gather | solution.py:64
  125.9 424.6 %while.20 = (s32[]{:T(128)}, bf16[352,1024]{1,0:T(8,128)(2,1)}, f32[352,1024]{1,0:T(8,128)S(1)}, f32[176,1024]{1,0:T(8,128)}, f32[]{:T(128)}, /*index=5*/s32[]{:...) while((s32[]{:T(128)}, bf16[352,1024]{1,0:T(8,128)(2,1)}, ...), condition=%wide.region_5.6_spmd.clone, body=%wide.region_4.5_spmd.clone.sunk | while | flops 383427808 | bytes 15525043 | solution.py:122
  134.4 10.3 %collective-permute-done.1 = bf16[352,1024]{1,0:T(8,128)(2,1)} collective-permute-done((bf16[352,1024]{1,0:T(8,128)(2,1)}, bf16[352,1024]{1,0:T(8,128)(2,1)}, u32[]{:S(2)}, u32[]{:S(2)}) %collective-permute-start.1) | collective-permute-done | bytes 720928 | tf_op jit(solution)/shard_map/while/body/eval_jaxpr/ppermute | solution.py:12
  146.0 6.5 %collective-permute-done = bf16[352,1024]{1,0:T(8,128)(2,1)} collective-permute-done((bf16[352,1024]{1,0:T(8,128)(2,1)S(1)}, bf16[352,1024]{1,0:T(8,128)(2,1)}, u32[]{:S(2)}, u32[]{:S(2)}) %collective-permute-start) | collective-permute-done | bytes 720928 | tf_op jit(solution)/shard_map/while/body/eval_jaxpr/ppermute | solution.py:12
  160.4 10.8 %collective-permute-done.1 = bf16[352,1024]{1,0:T(8,128)(2,1)} collective-permute-done((bf16[352,1024]{1,0:T(8,128)(2,1)}, bf16[352,1024]{1,0:T(8,128)(2,1)}, u32[]{:S(2)}, u32[]{:S(2)}) %collective-permute-start.1) | collective-permute-done | bytes 720928 | tf_op jit(solution)/shard_map/while/body/eval_jaxpr/ppermute | solution.py:12
  187.0 10.8 %collective-permute-done.1 = bf16[352,1024]{1,0:T(8,128)(2,1)} collective-permute-done((bf16[352,1024]{1,0:T(8,128)(2,1)}, bf16[352,1024]{1,0:T(8,128)(2,1)}, u32[]{:S(2)}, u32[]{:S(2)}) %collective-permute-start.1) | collective-permute-done | bytes 720928 | tf_op jit(solution)/shard_map/while/body/eval_jaxpr/ppermute | solution.py:12
  199.0 6.5 %collective-permute-done = bf16[352,1024]{1,0:T(8,128)(2,1)} collective-permute-done((bf16[352,1024]{1,0:T(8,128)(2,1)S(1)}, bf16[352,1024]{1,0:T(8,128)(2,1)}, u32[]{:S(2)}, u32[]{:S(2)}) %collective-permute-start) | collective-permute-done | bytes 720928 | tf_op jit(solution)/shard_map/while/body/eval_jaxpr/ppermute | solution.py:12
  213.5 10.8 %collective-permute-done.1 = bf16[352,1024]{1,0:T(8,128)(2,1)} collective-permute-done((bf16[352,1024]{1,0:T(8,128)(2,1)}, bf16[352,1024]{1,0:T(8,128)(2,1)}, u32[]{:S(2)}, u32[]{:S(2)}) %collective-permute-start.1) | collective-permute-done | bytes 720928 | tf_op jit(solution)/shard_map/while/body/eval_jaxpr/ppermute | solution.py:12
  225.6 6.5 %collective-permute-done = bf16[352,1024]{1,0:T(8,128)(2,1)} collective-permute-done((bf16[352,1024]{1,0:T(8,128)(2,1)S(1)}, bf16[352,1024]{1,0:T(8,128)(2,1)}, u32[]{:S(2)}, u32[]{:S(2)}) %collective-permute-start) | collective-permute-done | bytes 720928 | tf_op jit(solution)/shard_map/while/body/eval_jaxpr/ppermute | solution.py:12
  240.1 10.8 %collective-permute-done.1 = bf16[352,1024]{1,0:T(8,128)(2,1)} collective-permute-done((bf16[352,1024]{1,0:T(8,128)(2,1)}, bf16[352,1024]{1,0:T(8,128)(2,1)}, u32[]{:S(2)}, u32[]{:S(2)}) %collective-permute-start.1) | collective-permute-done | bytes 720928 | tf_op jit(solution)/shard_map/while/body/eval_jaxpr/ppermute | solution.py:12
  252.1 6.5 %collective-permute-done = bf16[352,1024]{1,0:T(8,128)(2,1)} collective-permute-done((bf16[352,1024]{1,0:T(8,128)(2,1)S(1)}, bf16[352,1024]{1,0:T(8,128)(2,1)}, u32[]{:S(2)}, u32[]{:S(2)}) %collective-permute-start) | collective-permute-done | bytes 720928 | tf_op jit(solution)/shard_map/while/body/eval_jaxpr/ppermute | solution.py:12
  266.6 10.8 %collective-permute-done.1 = bf16[352,1024]{1,0:T(8,128)(2,1)} collective-permute-done((bf16[352,1024]{1,0:T(8,128)(2,1)}, bf16[352,1024]{1,0:T(8,128)(2,1)}, u32[]{:S(2)}, u32[]{:S(2)}) %collective-permute-start.1) | collective-permute-done | bytes 720928 | tf_op jit(solution)/shard_map/while/body/eval_jaxpr/ppermute | solution.py:12
  293.1 10.8 %collective-permute-done.1 = bf16[352,1024]{1,0:T(8,128)(2,1)} collective-permute-done((bf16[352,1024]{1,0:T(8,128)(2,1)}, bf16[352,1024]{1,0:T(8,128)(2,1)}, u32[]{:S(2)}, u32[]{:S(2)}) %collective-permute-start.1) | collective-permute-done | bytes 720928 | tf_op jit(solution)/shard_map/while/body/eval_jaxpr/ppermute | solution.py:12
  319.7 10.8 %collective-permute-done.1 = bf16[352,1024]{1,0:T(8,128)(2,1)} collective-permute-done((bf16[352,1024]{1,0:T(8,128)(2,1)}, bf16[352,1024]{1,0:T(8,128)(2,1)}, u32[]{:S(2)}, u32[]{:S(2)}) %collective-permute-start.1) | collective-permute-done | bytes 720928 | tf_op jit(solution)/shard_map/while/body/eval_jaxpr/ppermute | solution.py:12
  346.2 10.8 %collective-permute-done.1 = bf16[352,1024]{1,0:T(8,128)(2,1)} collective-permute-done((bf16[352,1024]{1,0:T(8,128)(2,1)}, bf16[352,1024]{1,0:T(8,128)(2,1)}, u32[]{:S(2)}, u32[]{:S(2)}) %collective-permute-start.1) | collective-permute-done | bytes 720928 | tf_op jit(solution)/shard_map/while/body/eval_jaxpr/ppermute | solution.py:12
  372.7 10.8 %collective-permute-done.1 = bf16[352,1024]{1,0:T(8,128)(2,1)} collective-permute-done((bf16[352,1024]{1,0:T(8,128)(2,1)}, bf16[352,1024]{1,0:T(8,128)(2,1)}, u32[]{:S(2)}, u32[]{:S(2)}) %collective-permute-start.1) | collective-permute-done | bytes 720928 | tf_op jit(solution)/shard_map/while/body/eval_jaxpr/ppermute | solution.py:12
  399.3 10.8 %collective-permute-done.1 = bf16[352,1024]{1,0:T(8,128)(2,1)} collective-permute-done((bf16[352,1024]{1,0:T(8,128)(2,1)}, bf16[352,1024]{1,0:T(8,128)(2,1)}, u32[]{:S(2)}, u32[]{:S(2)}) %collective-permute-start.1) | collective-permute-done | bytes 720928 | tf_op jit(solution)/shard_map/while/body/eval_jaxpr/ppermute | solution.py:12
  425.8 10.8 %collective-permute-done.1 = bf16[352,1024]{1,0:T(8,128)(2,1)} collective-permute-done((bf16[352,1024]{1,0:T(8,128)(2,1)}, bf16[352,1024]{1,0:T(8,128)(2,1)}, u32[]{:S(2)}, u32[]{:S(2)}) %collective-permute-start.1) | collective-permute-done | bytes 720928 | tf_op jit(solution)/shard_map/while/body/eval_jaxpr/ppermute | solution.py:12
  452.4 10.8 %collective-permute-done.1 = bf16[352,1024]{1,0:T(8,128)(2,1)} collective-permute-done((bf16[352,1024]{1,0:T(8,128)(2,1)}, bf16[352,1024]{1,0:T(8,128)(2,1)}, u32[]{:S(2)}, u32[]{:S(2)}) %collective-permute-start.1) | collective-permute-done | bytes 720928 | tf_op jit(solution)/shard_map/while/body/eval_jaxpr/ppermute | solution.py:12
  478.9 10.8 %collective-permute-done.1 = bf16[352,1024]{1,0:T(8,128)(2,1)} collective-permute-done((bf16[352,1024]{1,0:T(8,128)(2,1)}, bf16[352,1024]{1,0:T(8,128)(2,1)}, u32[]{:S(2)}, u32[]{:S(2)}) %collective-permute-start.1) | collective-permute-done | bytes 720928 | tf_op jit(solution)/shard_map/while/body/eval_jaxpr/ppermute | solution.py:12
  505.5 10.8 %collective-permute-done.1 = bf16[352,1024]{1,0:T(8,128)(2,1)} collective-permute-done((bf16[352,1024]{1,0:T(8,128)(2,1)}, bf16[352,1024]{1,0:T(8,128)(2,1)}, u32[]{:S(2)}, u32[]{:S(2)}) %collective-permute-start.1) | collective-permute-done | bytes 720928 | tf_op jit(solution)/shard_map/while/body/eval_jaxpr/ppermute | solution.py:12
  532.0 10.8 %collective-permute-done.1 = bf16[352,1024]{1,0:T(8,128)(2,1)} collective-permute-done((bf16[352,1024]{1,0:T(8,128)(2,1)}, bf16[352,1024]{1,0:T(8,128)(2,1)}, u32[]{:S(2)}, u32[]{:S(2)}) %collective-permute-start.1) | collective-permute-done | bytes 720928 | tf_op jit(solution)/shard_map/while/body/eval_jaxpr/ppermute | solution.py:12
  561.6 62.6 %reduce-scatter.4.cloned.1.call-done = bf16[128,352]{1,0:T(8,128)(2,1)} async-done(((bf16[1024,352]{1,0:T(8,128)(2,1)}), bf16[128,352]{1,0:T(8,128)(2,1)}) %reduce-scatter.4.cloned.1.call-update) | async-done | bytes 90128
  (217 shorter events, 248.9 us)
Async XLA Ops:
  7.2 60.1 %all-gather.5.cloned.1.call-start = ((), (), s32[]{:S(2)}) async-start(), calls=%async_computation.2 | async-start | bytes 2359296 | tf_op jit(solution)/shard_map/all_gather | solution.py:65
  7.9 113.9 %all-gather.3.cloned.1.call-start = ((), (), s32[]{:S(2)}) async-start(), calls=%async_computation.1 | async-start | bytes 2359296 | tf_op jit(solution)/shard_map/all_gather | solution.py:64
  8.7 615.5 %reduce-scatter.4.cloned.1.call-start = ((), (), s32[]{:S(2)}) async-start(), calls=%async_computation.3 | async-start | bytes 884736
  131.6 13.1 %collective-permute-start.1 = (bf16[352,1024]{1,0:T(8,128)(2,1)}, bf16[352,1024]{1,0:T(8,128)(2,1)}, u32[]{:S(2)}, u32[]{:S(2)}) collective-permute-start(bf16[352,1024]{1,0:T(8,128)(2,1)} %fusion.49), channel_id=1, source_target_pairs={{0,8},{8,16},{16,24},{24,32},{32,40},{40,48},{48,56},{56,64},{64,7... | collective-permute-start | bytes 2162696 | tf_op jit(solution)/shard_map/while/body/eval_jaxpr/ppermute | solution.py:12
  131.6 20.9 %collective-permute-start = (bf16[352,1024]{1,0:T(8,128)(2,1)S(1)}, bf16[352,1024]{1,0:T(8,128)(2,1)}, u32[]{:S(2)}, u32[]{:S(2)}) collective-permute-start(bf16[352,1024]{1,0:T(8,128)(2,1)S(1)} %copy.16), channel_id=1, source_target_pairs={{0,8},{8,16},{16,24},{24,32},{32,40},{40,48},{48,56},{56,64},{64,7... | collective-permute-start | bytes 2162696 | tf_op jit(solution)/shard_map/while/body/eval_jaxpr/ppermute | solution.py:12
  158.1 13.1 %collective-permute-start.1 = (bf16[352,1024]{1,0:T(8,128)(2,1)}, bf16[352,1024]{1,0:T(8,128)(2,1)}, u32[]{:S(2)}, u32[]{:S(2)}) collective-permute-start(bf16[352,1024]{1,0:T(8,128)(2,1)} %fusion.49), channel_id=1, source_target_pairs={{0,8},{8,16},{16,24},{24,32},{32,40},{40,48},{48,56},{56,64},{64,7... | collective-permute-start | bytes 2162696 | tf_op jit(solution)/shard_map/while/body/eval_jaxpr/ppermute | solution.py:12
  158.1 20.9 %collective-permute-start = (bf16[352,1024]{1,0:T(8,128)(2,1)S(1)}, bf16[352,1024]{1,0:T(8,128)(2,1)}, u32[]{:S(2)}, u32[]{:S(2)}) collective-permute-start(bf16[352,1024]{1,0:T(8,128)(2,1)S(1)} %copy.16), channel_id=1, source_target_pairs={{0,8},{8,16},{16,24},{24,32},{32,40},{40,48},{48,56},{56,64},{64,7... | collective-permute-start | bytes 2162696 | tf_op jit(solution)/shard_map/while/body/eval_jaxpr/ppermute | solution.py:12
  184.6 13.1 %collective-permute-start.1 = (bf16[352,1024]{1,0:T(8,128)(2,1)}, bf16[352,1024]{1,0:T(8,128)(2,1)}, u32[]{:S(2)}, u32[]{:S(2)}) collective-permute-start(bf16[352,1024]{1,0:T(8,128)(2,1)} %fusion.49), channel_id=1, source_target_pairs={{0,8},{8,16},{16,24},{24,32},{32,40},{40,48},{48,56},{56,64},{64,7... | collective-permute-start | bytes 2162696 | tf_op jit(solution)/shard_map/while/body/eval_jaxpr/ppermute | solution.py:12
  184.6 20.9 %collective-permute-start = (bf16[352,1024]{1,0:T(8,128)(2,1)S(1)}, bf16[352,1024]{1,0:T(8,128)(2,1)}, u32[]{:S(2)}, u32[]{:S(2)}) collective-permute-start(bf16[352,1024]{1,0:T(8,128)(2,1)S(1)} %copy.16), channel_id=1, source_target_pairs={{0,8},{8,16},{16,24},{24,32},{32,40},{40,48},{48,56},{56,64},{64,7... | collective-permute-start | bytes 2162696 | tf_op jit(solution)/shard_map/while/body/eval_jaxpr/ppermute | solution.py:12
  211.2 13.1 %collective-permute-start.1 = (bf16[352,1024]{1,0:T(8,128)(2,1)}, bf16[352,1024]{1,0:T(8,128)(2,1)}, u32[]{:S(2)}, u32[]{:S(2)}) collective-permute-start(bf16[352,1024]{1,0:T(8,128)(2,1)} %fusion.49), channel_id=1, source_target_pairs={{0,8},{8,16},{16,24},{24,32},{32,40},{40,48},{48,56},{56,64},{64,7... | collective-permute-start | bytes 2162696 | tf_op jit(solution)/shard_map/while/body/eval_jaxpr/ppermute | solution.py:12
  211.2 20.9 %collective-permute-start = (bf16[352,1024]{1,0:T(8,128)(2,1)S(1)}, bf16[352,1024]{1,0:T(8,128)(2,1)}, u32[]{:S(2)}, u32[]{:S(2)}) collective-permute-start(bf16[352,1024]{1,0:T(8,128)(2,1)S(1)} %copy.16), channel_id=1, source_target_pairs={{0,8},{8,16},{16,24},{24,32},{32,40},{40,48},{48,56},{56,64},{64,7... | collective-permute-start | bytes 2162696 | tf_op jit(solution)/shard_map/while/body/eval_jaxpr/ppermute | solution.py:12
  237.7 13.1 %collective-permute-start.1 = (bf16[352,1024]{1,0:T(8,128)(2,1)}, bf16[352,1024]{1,0:T(8,128)(2,1)}, u32[]{:S(2)}, u32[]{:S(2)}) collective-permute-start(bf16[352,1024]{1,0:T(8,128)(2,1)} %fusion.49), channel_id=1, source_target_pairs={{0,8},{8,16},{16,24},{24,32},{32,40},{40,48},{48,56},{56,64},{64,7... | collective-permute-start | bytes 2162696 | tf_op jit(solution)/shard_map/while/body/eval_jaxpr/ppermute | solution.py:12
  237.7 20.9 %collective-permute-start = (bf16[352,1024]{1,0:T(8,128)(2,1)S(1)}, bf16[352,1024]{1,0:T(8,128)(2,1)}, u32[]{:S(2)}, u32[]{:S(2)}) collective-permute-start(bf16[352,1024]{1,0:T(8,128)(2,1)S(1)} %copy.16), channel_id=1, source_target_pairs={{0,8},{8,16},{16,24},{24,32},{32,40},{40,48},{48,56},{56,64},{64,7... | collective-permute-start | bytes 2162696 | tf_op jit(solution)/shard_map/while/body/eval_jaxpr/ppermute | solution.py:12
  264.2 20.9 %collective-permute-start = (bf16[352,1024]{1,0:T(8,128)(2,1)S(1)}, bf16[352,1024]{1,0:T(8,128)(2,1)}, u32[]{:S(2)}, u32[]{:S(2)}) collective-permute-start(bf16[352,1024]{1,0:T(8,128)(2,1)S(1)} %copy.16), channel_id=1, source_target_pairs={{0,8},{8,16},{16,24},{24,32},{32,40},{40,48},{48,56},{56,64},{64,7... | collective-permute-start | bytes 2162696 | tf_op jit(solution)/shard_map/while/body/eval_jaxpr/ppermute | solution.py:12
  290.8 20.9 %collective-permute-start = (bf16[352,1024]{1,0:T(8,128)(2,1)S(1)}, bf16[352,1024]{1,0:T(8,128)(2,1)}, u32[]{:S(2)}, u32[]{:S(2)}) collective-permute-start(bf16[352,1024]{1,0:T(8,128)(2,1)S(1)} %copy.16), channel_id=1, source_target_pairs={{0,8},{8,16},{16,24},{24,32},{32,40},{40,48},{48,56},{56,64},{64,7... | collective-permute-start | bytes 2162696 | tf_op jit(solution)/shard_map/while/body/eval_jaxpr/ppermute | solution.py:12
  317.3 20.9 %collective-permute-start = (bf16[352,1024]{1,0:T(8,128)(2,1)S(1)}, bf16[352,1024]{1,0:T(8,128)(2,1)}, u32[]{:S(2)}, u32[]{:S(2)}) collective-permute-start(bf16[352,1024]{1,0:T(8,128)(2,1)S(1)} %copy.16), channel_id=1, source_target_pairs={{0,8},{8,16},{16,24},{24,32},{32,40},{40,48},{48,56},{56,64},{64,7... | collective-permute-start | bytes 2162696 | tf_op jit(solution)/shard_map/while/body/eval_jaxpr/ppermute | solution.py:12
  343.9 20.9 %collective-permute-start = (bf16[352,1024]{1,0:T(8,128)(2,1)S(1)}, bf16[352,1024]{1,0:T(8,128)(2,1)}, u32[]{:S(2)}, u32[]{:S(2)}) collective-permute-start(bf16[352,1024]{1,0:T(8,128)(2,1)S(1)} %copy.16), channel_id=1, source_target_pairs={{0,8},{8,16},{16,24},{24,32},{32,40},{40,48},{48,56},{56,64},{64,7... | collective-permute-start | bytes 2162696 | tf_op jit(solution)/shard_map/while/body/eval_jaxpr/ppermute | solution.py:12
  370.4 20.9 %collective-permute-start = (bf16[352,1024]{1,0:T(8,128)(2,1)S(1)}, bf16[352,1024]{1,0:T(8,128)(2,1)}, u32[]{:S(2)}, u32[]{:S(2)}) collective-permute-start(bf16[352,1024]{1,0:T(8,128)(2,1)S(1)} %copy.16), channel_id=1, source_target_pairs={{0,8},{8,16},{16,24},{24,32},{32,40},{40,48},{48,56},{56,64},{64,7... | collective-permute-start | bytes 2162696 | tf_op jit(solution)/shard_map/while/body/eval_jaxpr/ppermute | solution.py:12
  397.0 20.9 %collective-permute-start = (bf16[352,1024]{1,0:T(8,128)(2,1)S(1)}, bf16[352,1024]{1,0:T(8,128)(2,1)}, u32[]{:S(2)}, u32[]{:S(2)}) collective-permute-start(bf16[352,1024]{1,0:T(8,128)(2,1)S(1)} %copy.16), channel_id=1, source_target_pairs={{0,8},{8,16},{16,24},{24,32},{32,40},{40,48},{48,56},{56,64},{64,7... | collective-permute-start | bytes 2162696 | tf_op jit(solution)/shard_map/while/body/eval_jaxpr/ppermute | solution.py:12
  423.5 20.9 %collective-permute-start = (bf16[352,1024]{1,0:T(8,128)(2,1)S(1)}, bf16[352,1024]{1,0:T(8,128)(2,1)}, u32[]{:S(2)}, u32[]{:S(2)}) collective-permute-start(bf16[352,1024]{1,0:T(8,128)(2,1)S(1)} %copy.16), channel_id=1, source_target_pairs={{0,8},{8,16},{16,24},{24,32},{32,40},{40,48},{48,56},{56,64},{64,7... | collective-permute-start | bytes 2162696 | tf_op jit(solution)/shard_map/while/body/eval_jaxpr/ppermute | solution.py:12
  450.0 20.9 %collective-permute-start = (bf16[352,1024]{1,0:T(8,128)(2,1)S(1)}, bf16[352,1024]{1,0:T(8,128)(2,1)}, u32[]{:S(2)}, u32[]{:S(2)}) collective-permute-start(bf16[352,1024]{1,0:T(8,128)(2,1)S(1)} %copy.16), channel_id=1, source_target_pairs={{0,8},{8,16},{16,24},{24,32},{32,40},{40,48},{48,56},{56,64},{64,7... | collective-permute-start | bytes 2162696 | tf_op jit(solution)/shard_map/while/body/eval_jaxpr/ppermute | solution.py:12
  476.6 20.9 %collective-permute-start = (bf16[352,1024]{1,0:T(8,128)(2,1)S(1)}, bf16[352,1024]{1,0:T(8,128)(2,1)}, u32[]{:S(2)}, u32[]{:S(2)}) collective-permute-start(bf16[352,1024]{1,0:T(8,128)(2,1)S(1)} %copy.16), channel_id=1, source_target_pairs={{0,8},{8,16},{16,24},{24,32},{32,40},{40,48},{48,56},{56,64},{64,7... | collective-permute-start | bytes 2162696 | tf_op jit(solution)/shard_map/while/body/eval_jaxpr/ppermute | solution.py:12
  503.1 20.9 %collective-permute-start = (bf16[352,1024]{1,0:T(8,128)(2,1)S(1)}, bf16[352,1024]{1,0:T(8,128)(2,1)}, u32[]{:S(2)}, u32[]{:S(2)}) collective-permute-start(bf16[352,1024]{1,0:T(8,128)(2,1)S(1)} %copy.16), channel_id=1, source_target_pairs={{0,8},{8,16},{16,24},{24,32},{32,40},{40,48},{48,56},{56,64},{64,7... | collective-permute-start | bytes 2162696 | tf_op jit(solution)/shard_map/while/body/eval_jaxpr/ppermute | solution.py:12
  529.7 20.9 %collective-permute-start = (bf16[352,1024]{1,0:T(8,128)(2,1)S(1)}, bf16[352,1024]{1,0:T(8,128)(2,1)}, u32[]{:S(2)}, u32[]{:S(2)}) collective-permute-start(bf16[352,1024]{1,0:T(8,128)(2,1)S(1)} %copy.16), channel_id=1, source_target_pairs={{0,8},{8,16},{16,24},{24,32},{32,40},{40,48},{48,56},{56,64},{64,7... | collective-permute-start | bytes 2162696 | tf_op jit(solution)/shard_map/while/body/eval_jaxpr/ppermute | solution.py:12
  (19 other events, 323.3 us)
Sparse Core Ops, SparseCore 0:
  10.2 57.0 all-gather.4
  69.5 52.3 all-gather.2
  557.3 66.8 reduce-scatter.3
where the time goes:
time: 636 us; the launch traced here: 632 us
  waiting for transfers between devices  448 us (70%)
  matrix products  93.8 us (15%)
  other arithmetic  50.7 us (8%)
  local copies, waits for them, and re-layouts  23.7 us (4%)
  between operations  13.9 us (2%)
    ppermute x32, waiting for transfers between devices, passed_along(): return lax.ppermute(value, axis, pairs)  276 us
    unnamed x4, waiting for transfers between devices  64 us
    all_gather x1, waiting for transfers between devices, body(): lax.all_gather(sentence_projector_matrix, 'tensor', axis=1, tiled=True)  56.4 us
    all_gather x1, waiting for transfers between devices, body(): lax.all_gather(picture_projector_matrix, 'tensor', axis=1, tiled=True)  52.2 us
    dot_general x16, matrix products, step(): jnp.einsum('mc,me->ce', pair_factor, block_z, preferred_element_type=jnp....  36.3 us
    dot_general x16, matrix products, image_tile(): jnp.einsum('me,ce->mc', block_z, cap_z, preferred_element_type=jnp.float32)  28.3 us
    convert_element_type x16, other arithmetic, step(): passed_along(carried.astype(jnp.bfloat16), 'dp', 1).astype(carried.dtype)  20.1 us
    dot_general x16, matrix products, step(): jnp.dot(pair_factor, cap_z, preferred_element_type=jnp.float32)  19.8 us
  transfers between devices with their start and end apart: 35, of which 35 were waited for; matrix products, arithmetic and copies ran while one was open for 10% of the time, Pallas kernels for 0%

commit v1 on v0

--- a/solution.py
+++ b/solution.py
@@ -61,7 +61,15 @@
     score_offset_term,
 ):
     full_img, full_cap = (
-        lax.all_gather(picture_projector_matrix, "tensor", axis=1, tiled=True),
+        jnp.concatenate(
+            lax.all_to_all(
+                jnp.stack([picture_projector_matrix for _ in range(lax.psum(1, "tensor"))], 0),
+                "tensor",
+                0,
+                0,
+            ),
+            1,
+        ),
         lax.all_gather(sentence_projector_matrix, "tensor", axis=1, tiled=True),
     )
     img_unit, img_scale = embed(picture_encoder_result, full_img)

time: 636 us -> 576 us (0.906)
  waiting for transfers between devices: 448 us -> 397 us
  other arithmetic: 50.7 us -> 26.7 us
  starting transfers between devices: 1.78 us -> 9.9 us
    all_gather x1 -> x0, waiting for transfers between devices: 52.2 us -> none  [body(): lax.all_gather(picture_projector_matrix, 'tensor', axis=1, tiled=True)]
    all_to_all x0 -> x1, waiting for transfers between devices: none -> 28.6 us  [body(): lax.all_to_all(jnp.stack([picture_projector_matrix for _ in range(lax.psu...]
    all_gather x1, waiting for transfers between devices: 56.4 us -> 30 us  [body(): lax.all_gather(sentence_projector_matrix, 'tensor', axis=1, tiled=True)]
    add x16, other arithmetic: 12.4 us -> 1.24 us  [scaling_factor(): other_begin_list + sentence_tally_later]
    div x16, other arithmetic: 12.3 us -> 1.24 us  [scaling_factor(): 1.0 / sentence_tally_later.astype(jnp.float32)]
    all_to_all x0 -> x1, starting transfers between devices: none -> 8.16 us  [body(): lax.all_to_all(jnp.stack([picture_projector_matrix for _ in range(lax.psu...]
    unnamed x4 -> x3, waiting for transfers between devices: 64 us -> 63.3 us
  transfers between devices with their start and end apart: 35 -> 35, of which waited for: 35 -> 35; matrix products, arithmetic and copies ran while one was open for 10% -> 12% of each run, Pallas kernels for 0% -> 0%
where the time goes in v1:
time: 576 us; the launch traced here: 573 us
  waiting for transfers between devices  397 us (69%)
  matrix products  97 us (17%)
  local copies, waits for them, and re-layouts  27.1 us (5%)
  other arithmetic  26.7 us (5%)
  between operations  14.2 us (2%)
  starting transfers between devices  9.9 us (2%)
    ppermute x32, waiting for transfers between devices, passed_along(): return lax.ppermute(value, axis, pairs)  276 us
    unnamed x3, waiting for transfers between devices  63.3 us
    dot_general x16, matrix products, step(): jnp.einsum('mc,me->ce', pair_factor, block_z, preferred_element_type=jnp....  36.2 us
    all_gather x1, waiting for transfers between devices, body(): lax.all_gather(sentence_projector_matrix, 'tensor', axis=1, tiled=True)  30 us
    all_to_all x1, waiting for transfers between devices, body(): lax.all_to_all(jnp.stack([picture_projector_matrix for _ in range(lax.psu...  28.6 us
    dot_general x16, matrix products, image_tile(): jnp.einsum('me,ce->mc', block_z, cap_z, preferred_element_type=jnp.float32)  28.4 us
    convert_element_type x16, other arithmetic, step(): passed_along(carried.astype(jnp.bfloat16), 'dp', 1).astype(carried.dtype)  20.1 us
    dot_general x16, matrix products, step(): jnp.dot(pair_factor, cap_z, preferred_element_type=jnp.float32)  19.8 us
  transfers between devices with their start and end apart: 35, of which 35 were waited for; matrix products, arithmetic and copies ran while one was open for 12% of the time, Pallas kernels for 0%

profile of v1, /device:TPU:0, one launch (start us, length us, event | category | flops | bytes accessed | tf_op | source)
XLA Modules:
  0.0 572.7 jit_solution(10570389925784544157)
XLA Ops:
  10.6 8.2 %all-to-all-start = ((bf16[8,1024,128]{1,2,0:T(8,128)(2,1)}), bf16[8,1024,128]{1,2,0:T(8,128)(2,1)}, u32[]{:S(2)}, u32[]{:S(2)}) async-start(bf16[8,1024,128]{1,2,0:T(8,128)(2,1)} %stack.2), calls=%async_computation | async-start | bytes 4194304 | tf_op jit(solution)/shard_map/all_to_all | solution.py:65
  19.5 28.6 %all-to-all-done = bf16[8,1024,128]{1,2,0:T(8,128)(2,1)} async-done(((bf16[8,1024,128]{1,2,0:T(8,128)(2,1)}), bf16[8,1024,128]{1,2,0:T(8,128)(2,1)}, u32[]{:S(2)}, u32[]{:S(2)}) %all-to-all-start) | async-done | bytes 2097184 | tf_op jit(solution)/shard_map/all_to_all | solution.py:65
  52.9 30.0 %all-gather.2.cloned.1.call-done = bf16[1024,1024]{1,0:T(8,128)(2,1)} async-done(((bf16[1024,128]{1,0:T(8,128)(2,1)}), bf16[1024,1024]{1,0:T(8,128)(2,1)}) %all-gather.2.cloned.1.call-update) | async-done | bytes 2097168 | tf_op jit(solution)/shard_map/all_gather | solution.py:73
  86.1 402.7 %while.20 = (s32[]{:T(128)}, bf16[352,1024]{1,0:T(8,128)(2,1)}, f32[352,1024]{1,0:T(8,128)S(1)}, f32[176,1024]{1,0:T(8,128)}, f32[]{:T(128)}, /*index=5*/s32[]{:...) while((s32[]{:T(128)}, bf16[352,1024]{1,0:T(8,128)(2,1)}, ...), condition=%wide.region_5.6_spmd.clone, body=%wide.region_4.5_spmd.clone.sunk | while | flops 383427808 | bytes 15525043 | solution.py:130
  93.3 10.3 %collective-permute-done.1 = bf16[352,1024]{1,0:T(8,128)(2,1)} collective-permute-done((bf16[352,1024]{1,0:T(8,128)(2,1)}, bf16[352,1024]{1,0:T(8,128)(2,1)}, u32[]{:S(2)}, u32[]{:S(2)}) %collective-permute-start.1) | collective-permute-done | bytes 720928 | tf_op jit(solution)/shard_map/while/body/eval_jaxpr/ppermute | solution.py:12
  118.0 10.8 %collective-permute-done.1 = bf16[352,1024]{1,0:T(8,128)(2,1)} collective-permute-done((bf16[352,1024]{1,0:T(8,128)(2,1)}, bf16[352,1024]{1,0:T(8,128)(2,1)}, u32[]{:S(2)}, u32[]{:S(2)}) %collective-permute-start.1) | collective-permute-done | bytes 720928 | tf_op jit(solution)/shard_map/while/body/eval_jaxpr/ppermute | solution.py:12
  143.1 10.8 %collective-permute-done.1 = bf16[352,1024]{1,0:T(8,128)(2,1)} collective-permute-done((bf16[352,1024]{1,0:T(8,128)(2,1)}, bf16[352,1024]{1,0:T(8,128)(2,1)}, u32[]{:S(2)}, u32[]{:S(2)}) %collective-permute-start.1) | collective-permute-done | bytes 720928 | tf_op jit(solution)/shard_map/while/body/eval_jaxpr/ppermute | solution.py:12
  155.2 6.5 %collective-permute-done = bf16[352,1024]{1,0:T(8,128)(2,1)} collective-permute-done((bf16[352,1024]{1,0:T(8,128)(2,1)S(1)}, bf16[352,1024]{1,0:T(8,128)(2,1)}, u32[]{:S(2)}, u32[]{:S(2)}) %collective-permute-start) | collective-permute-done | bytes 720928 | tf_op jit(solution)/shard_map/while/body/eval_jaxpr/ppermute | solution.py:12
  168.3 10.8 %collective-permute-done.1 = bf16[352,1024]{1,0:T(8,128)(2,1)} collective-permute-done((bf16[352,1024]{1,0:T(8,128)(2,1)}, bf16[352,1024]{1,0:T(8,128)(2,1)}, u32[]{:S(2)}, u32[]{:S(2)}) %collective-permute-start.1) | collective-permute-done | bytes 720928 | tf_op jit(solution)/shard_map/while/body/eval_jaxpr/ppermute | solution.py:12
  180.3 6.5 %collective-permute-done = bf16[352,1024]{1,0:T(8,128)(2,1)} collective-permute-done((bf16[352,1024]{1,0:T(8,128)(2,1)S(1)}, bf16[352,1024]{1,0:T(8,128)(2,1)}, u32[]{:S(2)}, u32[]{:S(2)}) %collective-permute-start) | collective-permute-done | bytes 720928 | tf_op jit(solution)/shard_map/while/body/eval_jaxpr/ppermute | solution.py:12
  193.4 10.8 %collective-permute-done.1 = bf16[352,1024]{1,0:T(8,128)(2,1)} collective-permute-done((bf16[352,1024]{1,0:T(8,128)(2,1)}, bf16[352,1024]{1,0:T(8,128)(2,1)}, u32[]{:S(2)}, u32[]{:S(2)}) %collective-permute-start.1) | collective-permute-done | bytes 720928 | tf_op jit(solution)/shard_map/while/body/eval_jaxpr/ppermute | solution.py:12
  218.6 10.8 %collective-permute-done.1 = bf16[352,1024]{1,0:T(8,128)(2,1)} collective-permute-done((bf16[352,1024]{1,0:T(8,128)(2,1)}, bf16[352,1024]{1,0:T(8,128)(2,1)}, u32[]{:S(2)}, u32[]{:S(2)}) %collective-permute-start.1) | collective-permute-done | bytes 720928 | tf_op jit(solution)/shard_map/while/body/eval_jaxpr/ppermute | solution.py:12
  243.8 10.8 %collective-permute-done.1 = bf16[352,1024]{1,0:T(8,128)(2,1)} collective-permute-done((bf16[352,1024]{1,0:T(8,128)(2,1)}, bf16[352,1024]{1,0:T(8,128)(2,1)}, u32[]{:S(2)}, u32[]{:S(2)}) %collective-permute-start.1) | collective-permute-done | bytes 720928 | tf_op jit(solution)/shard_map/while/body/eval_jaxpr/ppermute | solution.py:12
  268.9 10.8 %collective-permute-done.1 = bf16[352,1024]{1,0:T(8,128)(2,1)} collective-permute-done((bf16[352,1024]{1,0:T(8,128)(2,1)}, bf16[352,1024]{1,0:T(8,128)(2,1)}, u32[]{:S(2)}, u32[]{:S(2)}) %collective-permute-start.1) | collective-permute-done | bytes 720928 | tf_op jit(solution)/shard_map/while/body/eval_jaxpr/ppermute | solution.py:12
  281.0 6.5 %collective-permute-done = bf16[352,1024]{1,0:T(8,128)(2,1)} collective-permute-done((bf16[352,1024]{1,0:T(8,128)(2,1)S(1)}, bf16[352,1024]{1,0:T(8,128)(2,1)}, u32[]{:S(2)}, u32[]{:S(2)}) %collective-permute-start) | collective-permute-done | bytes 720928 | tf_op jit(solution)/shard_map/while/body/eval_jaxpr/ppermute | solution.py:12
  294.1 10.8 %collective-permute-done.1 = bf16[352,1024]{1,0:T(8,128)(2,1)} collective-permute-done((bf16[352,1024]{1,0:T(8,128)(2,1)}, bf16[352,1024]{1,0:T(8,128)(2,1)}, u32[]{:S(2)}, u32[]{:S(2)}) %collective-permute-start.1) | collective-permute-done | bytes 720928 | tf_op jit(solution)/shard_map/while/body/eval_jaxpr/ppermute | solution.py:12
  319.3 10.8 %collective-permute-done.1 = bf16[352,1024]{1,0:T(8,128)(2,1)} collective-permute-done((bf16[352,1024]{1,0:T(8,128)(2,1)}, bf16[352,1024]{1,0:T(8,128)(2,1)}, u32[]{:S(2)}, u32[]{:S(2)}) %collective-permute-start.1) | collective-permute-done | bytes 720928 | tf_op jit(solution)/shard_map/while/body/eval_jaxpr/ppermute | solution.py:12
  344.4 10.8 %collective-permute-done.1 = bf16[352,1024]{1,0:T(8,128)(2,1)} collective-permute-done((bf16[352,1024]{1,0:T(8,128)(2,1)}, bf16[352,1024]{1,0:T(8,128)(2,1)}, u32[]{:S(2)}, u32[]{:S(2)}) %collective-permute-start.1) | collective-permute-done | bytes 720928 | tf_op jit(solution)/shard_map/while/body/eval_jaxpr/ppermute | solution.py:12
  369.6 10.8 %collective-permute-done.1 = bf16[352,1024]{1,0:T(8,128)(2,1)} collective-permute-done((bf16[352,1024]{1,0:T(8,128)(2,1)}, bf16[352,1024]{1,0:T(8,128)(2,1)}, u32[]{:S(2)}, u32[]{:S(2)}) %collective-permute-start.1) | collective-permute-done | bytes 720928 | tf_op jit(solution)/shard_map/while/body/eval_jaxpr/ppermute | solution.py:12
  394.7 10.8 %collective-permute-done.1 = bf16[352,1024]{1,0:T(8,128)(2,1)} collective-permute-done((bf16[352,1024]{1,0:T(8,128)(2,1)}, bf16[352,1024]{1,0:T(8,128)(2,1)}, u32[]{:S(2)}, u32[]{:S(2)}) %collective-permute-start.1) | collective-permute-done | bytes 720928 | tf_op jit(solution)/shard_map/while/body/eval_jaxpr/ppermute | solution.py:12
  419.9 10.8 %collective-permute-done.1 = bf16[352,1024]{1,0:T(8,128)(2,1)} collective-permute-done((bf16[352,1024]{1,0:T(8,128)(2,1)}, bf16[352,1024]{1,0:T(8,128)(2,1)}, u32[]{:S(2)}, u32[]{:S(2)}) %collective-permute-start.1) | collective-permute-done | bytes 720928 | tf_op jit(solution)/shard_map/while/body/eval_jaxpr/ppermute | solution.py:12
  445.1 10.8 %collective-permute-done.1 = bf16[352,1024]{1,0:T(8,128)(2,1)} collective-permute-done((bf16[352,1024]{1,0:T(8,128)(2,1)}, bf16[352,1024]{1,0:T(8,128)(2,1)}, u32[]{:S(2)}, u32[]{:S(2)}) %collective-permute-start.1) | collective-permute-done | bytes 720928 | tf_op jit(solution)/shard_map/while/body/eval_jaxpr/ppermute | solution.py:12
  470.2 10.8 %collective-permute-done.1 = bf16[352,1024]{1,0:T(8,128)(2,1)} collective-permute-done((bf16[352,1024]{1,0:T(8,128)(2,1)}, bf16[352,1024]{1,0:T(8,128)(2,1)}, u32[]{:S(2)}, u32[]{:S(2)}) %collective-permute-start.1) | collective-permute-done | bytes 720928 | tf_op jit(solution)/shard_map/while/body/eval_jaxpr/ppermute | solution.py:12
  501.7 62.6 %reduce-scatter.4.cloned.1.call-done = bf16[128,352]{1,0:T(8,128)(2,1)} async-done(((bf16[1024,352]{1,0:T(8,128)(2,1)}), bf16[128,352]{1,0:T(8,128)(2,1)}) %reduce-scatter.4.cloned.1.call-update) | async-done | bytes 90128
  (220 shorter events, 237.2 us)
Async XLA Ops:
  7.2 75.7 %all-gather.2.cloned.1.call-start = ((), (), s32[]{:S(2)}) async-start(), calls=%async_computation.2 | async-start | bytes 2359296 | tf_op jit(solution)/shard_map/all_gather | solution.py:73
  10.6 37.4 %all-to-all-start = ((bf16[8,1024,128]{1,2,0:T(8,128)(2,1)}), bf16[8,1024,128]{1,2,0:T(8,128)(2,1)}, u32[]{:S(2)}, u32[]{:S(2)}) async-start(bf16[8,1024,128]{1,2,0:T(8,128)(2,1)} %stack.2), calls=%async_computation | async-start | bytes 4194304 | tf_op jit(solution)/shard_map/all_to_all | solution.py:65
  18.8 545.5 %reduce-scatter.4.cloned.1.call-start = ((), (), s32[]{:S(2)}) async-start(), calls=%async_computation.3 | async-start | bytes 884736
  90.4 13.1 %collective-permute-start.1 = (bf16[352,1024]{1,0:T(8,128)(2,1)}, bf16[352,1024]{1,0:T(8,128)(2,1)}, u32[]{:S(2)}, u32[]{:S(2)}) collective-permute-start(bf16[352,1024]{1,0:T(8,128)(2,1)} %fusion.49), channel_id=1, source_target_pairs={{0,8},{8,16},{16,24},{24,32},{32,40},{40,48},{48,56},{56,64},{64,7... | collective-permute-start | bytes 2162696 | tf_op jit(solution)/shard_map/while/body/eval_jaxpr/ppermute | solution.py:12
  90.5 20.9 %collective-permute-start = (bf16[352,1024]{1,0:T(8,128)(2,1)S(1)}, bf16[352,1024]{1,0:T(8,128)(2,1)}, u32[]{:S(2)}, u32[]{:S(2)}) collective-permute-start(bf16[352,1024]{1,0:T(8,128)(2,1)S(1)} %copy.18), channel_id=1, source_target_pairs={{0,8},{8,16},{16,24},{24,32},{32,40},{40,48},{48,56},{56,64},{64,7... | collective-permute-start | bytes 2162696 | tf_op jit(solution)/shard_map/while/body/eval_jaxpr/ppermute | solution.py:12
  115.6 13.1 %collective-permute-start.1 = (bf16[352,1024]{1,0:T(8,128)(2,1)}, bf16[352,1024]{1,0:T(8,128)(2,1)}, u32[]{:S(2)}, u32[]{:S(2)}) collective-permute-start(bf16[352,1024]{1,0:T(8,128)(2,1)} %fusion.49), channel_id=1, source_target_pairs={{0,8},{8,16},{16,24},{24,32},{32,40},{40,48},{48,56},{56,64},{64,7... | collective-permute-start | bytes 2162696 | tf_op jit(solution)/shard_map/while/body/eval_jaxpr/ppermute | solution.py:12
  115.6 20.9 %collective-permute-start = (bf16[352,1024]{1,0:T(8,128)(2,1)S(1)}, bf16[352,1024]{1,0:T(8,128)(2,1)}, u32[]{:S(2)}, u32[]{:S(2)}) collective-permute-start(bf16[352,1024]{1,0:T(8,128)(2,1)S(1)} %copy.18), channel_id=1, source_target_pairs={{0,8},{8,16},{16,24},{24,32},{32,40},{40,48},{48,56},{56,64},{64,7... | collective-permute-start | bytes 2162696 | tf_op jit(solution)/shard_map/while/body/eval_jaxpr/ppermute | solution.py:12
  140.8 13.1 %collective-permute-start.1 = (bf16[352,1024]{1,0:T(8,128)(2,1)}, bf16[352,1024]{1,0:T(8,128)(2,1)}, u32[]{:S(2)}, u32[]{:S(2)}) collective-permute-start(bf16[352,1024]{1,0:T(8,128)(2,1)} %fusion.49), channel_id=1, source_target_pairs={{0,8},{8,16},{16,24},{24,32},{32,40},{40,48},{48,56},{56,64},{64,7... | collective-permute-start | bytes 2162696 | tf_op jit(solution)/shard_map/while/body/eval_jaxpr/ppermute | solution.py:12
  140.8 20.9 %collective-permute-start = (bf16[352,1024]{1,0:T(8,128)(2,1)S(1)}, bf16[352,1024]{1,0:T(8,128)(2,1)}, u32[]{:S(2)}, u32[]{:S(2)}) collective-permute-start(bf16[352,1024]{1,0:T(8,128)(2,1)S(1)} %copy.18), channel_id=1, source_target_pairs={{0,8},{8,16},{16,24},{24,32},{32,40},{40,48},{48,56},{56,64},{64,7... | collective-permute-start | bytes 2162696 | tf_op jit(solution)/shard_map/while/body/eval_jaxpr/ppermute | solution.py:12
  165.9 13.1 %collective-permute-start.1 = (bf16[352,1024]{1,0:T(8,128)(2,1)}, bf16[352,1024]{1,0:T(8,128)(2,1)}, u32[]{:S(2)}, u32[]{:S(2)}) collective-permute-start(bf16[352,1024]{1,0:T(8,128)(2,1)} %fusion.49), channel_id=1, source_target_pairs={{0,8},{8,16},{16,24},{24,32},{32,40},{40,48},{48,56},{56,64},{64,7... | collective-permute-start | bytes 2162696 | tf_op jit(solution)/shard_map/while/body/eval_jaxpr/ppermute | solution.py:12
  165.9 20.9 %collective-permute-start = (bf16[352,1024]{1,0:T(8,128)(2,1)S(1)}, bf16[352,1024]{1,0:T(8,128)(2,1)}, u32[]{:S(2)}, u32[]{:S(2)}) collective-permute-start(bf16[352,1024]{1,0:T(8,128)(2,1)S(1)} %copy.18), channel_id=1, source_target_pairs={{0,8},{8,16},{16,24},{24,32},{32,40},{40,48},{48,56},{56,64},{64,7... | collective-permute-start | bytes 2162696 | tf_op jit(solution)/shard_map/while/body/eval_jaxpr/ppermute | solution.py:12
  191.1 20.9 %collective-permute-start = (bf16[352,1024]{1,0:T(8,128)(2,1)S(1)}, bf16[352,1024]{1,0:T(8,128)(2,1)}, u32[]{:S(2)}, u32[]{:S(2)}) collective-permute-start(bf16[352,1024]{1,0:T(8,128)(2,1)S(1)} %copy.18), channel_id=1, source_target_pairs={{0,8},{8,16},{16,24},{24,32},{32,40},{40,48},{48,56},{56,64},{64,7... | collective-permute-start | bytes 2162696 | tf_op jit(solution)/shard_map/while/body/eval_jaxpr/ppermute | solution.py:12
  216.3 20.9 %collective-permute-start = (bf16[352,1024]{1,0:T(8,128)(2,1)S(1)}, bf16[352,1024]{1,0:T(8,128)(2,1)}, u32[]{:S(2)}, u32[]{:S(2)}) collective-permute-start(bf16[352,1024]{1,0:T(8,128)(2,1)S(1)} %copy.18), channel_id=1, source_target_pairs={{0,8},{8,16},{16,24},{24,32},{32,40},{40,48},{48,56},{56,64},{64,7... | collective-permute-start | bytes 2162696 | tf_op jit(solution)/shard_map/while/body/eval_jaxpr/ppermute | solution.py:12
  241.4 20.9 %collective-permute-start = (bf16[352,1024]{1,0:T(8,128)(2,1)S(1)}, bf16[352,1024]{1,0:T(8,128)(2,1)}, u32[]{:S(2)}, u32[]{:S(2)}) collective-permute-start(bf16[352,1024]{1,0:T(8,128)(2,1)S(1)} %copy.18), channel_id=1, source_target_pairs={{0,8},{8,16},{16,24},{24,32},{32,40},{40,48},{48,56},{56,64},{64,7... | collective-permute-start | bytes 2162696 | tf_op jit(solution)/shard_map/while/body/eval_jaxpr/ppermute | solution.py:12
  266.6 20.9 %collective-permute-start = (bf16[352,1024]{1,0:T(8,128)(2,1)S(1)}, bf16[352,1024]{1,0:T(8,128)(2,1)}, u32[]{:S(2)}, u32[]{:S(2)}) collective-permute-start(bf16[352,1024]{1,0:T(8,128)(2,1)S(1)} %copy.18), channel_id=1, source_target_pairs={{0,8},{8,16},{16,24},{24,32},{32,40},{40,48},{48,56},{56,64},{64,7... | collective-permute-start | bytes 2162696 | tf_op jit(solution)/shard_map/while/body/eval_jaxpr/ppermute | solution.py:12
  291.8 20.9 %collective-permute-start = (bf16[352,1024]{1,0:T(8,128)(2,1)S(1)}, bf16[352,1024]{1,0:T(8,128)(2,1)}, u32[]{:S(2)}, u32[]{:S(2)}) collective-permute-start(bf16[352,1024]{1,0:T(8,128)(2,1)S(1)} %copy.18), channel_id=1, source_target_pairs={{0,8},{8,16},{16,24},{24,32},{32,40},{40,48},{48,56},{56,64},{64,7... | collective-permute-start | bytes 2162696 | tf_op jit(solution)/shard_map/while/body/eval_jaxpr/ppermute | solution.py:12
  316.9 20.9 %collective-permute-start = (bf16[352,1024]{1,0:T(8,128)(2,1)S(1)}, bf16[352,1024]{1,0:T(8,128)(2,1)}, u32[]{:S(2)}, u32[]{:S(2)}) collective-permute-start(bf16[352,1024]{1,0:T(8,128)(2,1)S(1)} %copy.18), channel_id=1, source_target_pairs={{0,8},{8,16},{16,24},{24,32},{32,40},{40,48},{48,56},{56,64},{64,7... | collective-permute-start | bytes 2162696 | tf_op jit(solution)/shard_map/while/body/eval_jaxpr/ppermute | solution.py:12
  342.1 20.9 %collective-permute-start = (bf16[352,1024]{1,0:T(8,128)(2,1)S(1)}, bf16[352,1024]{1,0:T(8,128)(2,1)}, u32[]{:S(2)}, u32[]{:S(2)}) collective-permute-start(bf16[352,1024]{1,0:T(8,128)(2,1)S(1)} %copy.18), channel_id=1, source_target_pairs={{0,8},{8,16},{16,24},{24,32},{32,40},{40,48},{48,56},{56,64},{64,7... | collective-permute-start | bytes 2162696 | tf_op jit(solution)/shard_map/while/body/eval_jaxpr/ppermute | solution.py:12
  367.2 20.9 %collective-permute-start = (bf16[352,1024]{1,0:T(8,128)(2,1)S(1)}, bf16[352,1024]{1,0:T(8,128)(2,1)}, u32[]{:S(2)}, u32[]{:S(2)}) collective-permute-start(bf16[352,1024]{1,0:T(8,128)(2,1)S(1)} %copy.18), channel_id=1, source_target_pairs={{0,8},{8,16},{16,24},{24,32},{32,40},{40,48},{48,56},{56,64},{64,7... | collective-permute-start | bytes 2162696 | tf_op jit(solution)/shard_map/while/body/eval_jaxpr/ppermute | solution.py:12
  392.4 20.9 %collective-permute-start = (bf16[352,1024]{1,0:T(8,128)(2,1)S(1)}, bf16[352,1024]{1,0:T(8,128)(2,1)}, u32[]{:S(2)}, u32[]{:S(2)}) collective-permute-start(bf16[352,1024]{1,0:T(8,128)(2,1)S(1)} %copy.18), channel_id=1, source_target_pairs={{0,8},{8,16},{16,24},{24,32},{32,40},{40,48},{48,56},{56,64},{64,7... | collective-permute-start | bytes 2162696 | tf_op jit(solution)/shard_map/while/body/eval_jaxpr/ppermute | solution.py:12
  417.6 20.9 %collective-permute-start = (bf16[352,1024]{1,0:T(8,128)(2,1)S(1)}, bf16[352,1024]{1,0:T(8,128)(2,1)}, u32[]{:S(2)}, u32[]{:S(2)}) collective-permute-start(bf16[352,1024]{1,0:T(8,128)(2,1)S(1)} %copy.18), channel_id=1, source_target_pairs={{0,8},{8,16},{16,24},{24,32},{32,40},{40,48},{48,56},{56,64},{64,7... | collective-permute-start | bytes 2162696 | tf_op jit(solution)/shard_map/while/body/eval_jaxpr/ppermute | solution.py:12
  442.7 13.1 %collective-permute-start.1 = (bf16[352,1024]{1,0:T(8,128)(2,1)}, bf16[352,1024]{1,0:T(8,128)(2,1)}, u32[]{:S(2)}, u32[]{:S(2)}) collective-permute-start(bf16[352,1024]{1,0:T(8,128)(2,1)} %fusion.49), channel_id=1, source_target_pairs={{0,8},{8,16},{16,24},{24,32},{32,40},{40,48},{48,56},{56,64},{64,7... | collective-permute-start | bytes 2162696 | tf_op jit(solution)/shard_map/while/body/eval_jaxpr/ppermute | solution.py:12
  442.7 20.9 %collective-permute-start = (bf16[352,1024]{1,0:T(8,128)(2,1)S(1)}, bf16[352,1024]{1,0:T(8,128)(2,1)}, u32[]{:S(2)}, u32[]{:S(2)}) collective-permute-start(bf16[352,1024]{1,0:T(8,128)(2,1)S(1)} %copy.18), channel_id=1, source_target_pairs={{0,8},{8,16},{16,24},{24,32},{32,40},{40,48},{48,56},{56,64},{64,7... | collective-permute-start | bytes 2162696 | tf_op jit(solution)/shard_map/while/body/eval_jaxpr/ppermute | solution.py:12
  467.9 20.9 %collective-permute-start = (bf16[352,1024]{1,0:T(8,128)(2,1)S(1)}, bf16[352,1024]{1,0:T(8,128)(2,1)}, u32[]{:S(2)}, u32[]{:S(2)}) collective-permute-start(bf16[352,1024]{1,0:T(8,128)(2,1)S(1)} %copy.18), channel_id=1, source_target_pairs={{0,8},{8,16},{16,24},{24,32},{32,40},{40,48},{48,56},{56,64},{64,7... | collective-permute-start | bytes 2162696 | tf_op jit(solution)/shard_map/while/body/eval_jaxpr/ppermute | solution.py:12
  (20 other events, 234.0 us)
Sparse Core Ops, SparseCore 0:
  10.2 72.6 all-gather.1
  497.3 66.8 reduce-scatter.3
